TPU v7x, 32 devices: a whole 2x2x4 slice. The times are simulated.
32 devices in a mesh: fsdp: 4 (over y, x), tp: 8 (over z, core).
Axes of the slice: x: 2, y: 2, z: 4, core: 2. Of those that a mesh axis runs over, the one named last changes fastest.
Arguments:
- prefix_states: bfloat16 [16384, 8192], P('fsdp', 'tp'), may hold values from -40 to 40
- new_states: bfloat16 [64, 8192], P('fsdp', 'tp'), may hold values from -40 to 40
- w_query: bfloat16 [8192, 8192], P('tp', 'fsdp'), may hold values from -0.09375 to 0.09375
- w_keyvalue: bfloat16 [8192, 2048], P('tp', 'fsdp'), may hold values from -0.03125 to 0.03125
- w_output: bfloat16 [8192, 8192], P('tp', 'fsdp'), may hold values from -0.25 to 0.25
- lengths: int32 [4, 4], P('fsdp'), may hold values from 1 to 1024, 3072 in all within a row
Outputs:
- kv_cache: bfloat16 [16384, 2048], P('fsdp', 'tp')
- mixed: bfloat16 [64, 8192], P('fsdp', 'tp')
Inputs may be any that keep to these rules, and one draw needn't show every extreme that they name: `lengths`: in every group some sequence has length 1024.
All inputs are finite; a program needn't handle non-finite values.
Results may differ from a plain program's by a relative error of at most 0.02.
Values may be sent and summed in bfloat16 or wider, within the bound.
A program may use at most 128 MiB of HBM per device.

v0:
```python
import functools

import jax
import jax.numpy as jnp
from jax import lax
from jax.experimental import pallas as pl
from jax.experimental.pallas import tpu as pltpu
from jax.sharding import PartitionSpec as P

HD = 128
NSEQ = 4
L = 1024
STEPS = 4
SKEW = 2
MESH = pl.DeviceIdType.MESH
VMEM = pl.BlockSpec(memory_space=pltpu.VMEM)


theta_base = 500000.0
masked_score = -1e30


def partner(block, axis, apart):
    count = lax.axis_size(axis)
    route = []
    for low in range(count):
        high = low | 1 << apart
        if high != low and high < count:
            route += [(low, high), (high, low)]
    return lax.ppermute(block, axis, route)


def rotate(values, positions):
    half_dim = values.shape[-1] // 2
    frequency = theta_base ** (-2.0 * jnp.arange(half_dim, dtype=jnp.float32) / values.shape[-1])
    angles = positions[:, None, None] * frequency[None, None, :]
    cosine = jnp.cos(angles)
    sine_part = jnp.sin(angles)
    lower_half = values[..., :half_dim]
    upper_half = values[..., half_dim:]
    return jnp.concatenate(
        [
            lower_half * cosine - upper_half * sine_part,
            upper_half * cosine + lower_half * sine_part,
        ],
        axis=-1,
    )


def flip(number, other, bits):
    result = 0
    for b in range(bits):
        one = lax.rem(lax.div(number, 1 << b), 2)
        two = lax.rem(lax.div(other, 1 << b), 2) if not isinstance(other, int) else (other >> b) & 1
        result = result + (one + two - 2 * one * two) * (1 << b)
    return result


def relay(f, t, groups, members, x_ref, x_all, near_out, near_in, far_in, sems):
    x_send, x_recv, near_send, near_recv, far_send, far_recv = sems
    rows = x_ref.shape[0]
    share = members // groups

    def across(j):
        return lax.rem(f + j, groups)

    def along(i):
        return lax.rem(t + i, members)

    def x_copy(j, slot):
        return pltpu.make_async_remote_copy(
            src_ref=x_ref, dst_ref=x_all.at[slot], send_sem=x_send.at[j], recv_sem=x_recv.at[slot],
            device_id=(across(j), t), device_id_type=MESH)

    def near_copy(j, slot):
        return pltpu.make_async_remote_copy(
            src_ref=near_out.at[:, pl.ds(pl.multiple_of(across(j) * rows, rows), rows)],
            dst_ref=near_in.at[slot], send_sem=near_send.at[j], recv_sem=near_recv.at[slot],
            device_id=(across(j), t), device_id_type=MESH)

    def far_copy(i, slot):
        to = along(i)
        return pltpu.make_async_remote_copy(
            src_ref=near_in.at[lax.div(to, share), lax.rem(to, share)],
            dst_ref=far_in.at[slot], send_sem=far_send.at[i], recv_sem=far_recv.at[slot],
            device_id=(f, to), device_id_type=MESH)

    def gather():
        for j in range(1, groups):
            x_copy(j, f).start()
        x_all[f] = x_ref[...]

    def multiply(weights):
        for j in range(1, groups):
            x_copy(j, across(j)).wait_recv()
        x = x_all[...].reshape(groups * rows, x_ref.shape[1])
        for h in range(share):
            base = 0
            for w_ref in weights:
                width = w_ref.shape[1] // share
                near_out[h, :, base:base + width] = jnp.dot(
                    x, w_ref[:, h * width:(h + 1) * width], preferred_element_type=jnp.float32
                ).astype(near_out.dtype)
                base += width
        for j in range(1, groups):
            near_copy(j, f).start()
        near_in[f] = near_out[:, pl.ds(pl.multiple_of(f * rows, rows), rows)]

    def scatter():
        for j in range(1, groups):
            near_copy(j, across(j)).wait_recv()
        for i in range(1, members):
            far_copy(i, t).start()
        far_in[t] = near_in[lax.div(t, share), lax.rem(t, share)]

    def collect():
        for i in range(1, members):
            far_copy(i, along(i)).wait_recv()
        result = far_in[0].astype(jnp.float32)
        for source in range(1, members):
            result += far_in[source].astype(jnp.float32)
        return result

    def drain():
        for j in range(1, groups):
            x_copy(j, f).wait_send()
            near_copy(j, f).wait_send()
        for i in range(1, members):
            far_copy(i, t).wait_send()

    return gather, multiply, scatter, collect, drain


def relay_scratch(groups, members, rows, depth, columns):
    share = members // groups
    return [
        pltpu.VMEM((groups, rows, depth), jnp.bfloat16),
        pltpu.VMEM((share, groups * rows, columns), jnp.bfloat16),
        pltpu.VMEM((groups, share, rows, columns), jnp.bfloat16),
        pltpu.VMEM((members, rows, columns), jnp.bfloat16),
    ] + [pltpu.SemaphoreType.DMA((n,)) for n in (groups, groups, groups, groups, members, members)]


def cache_kernel(groups, chips, pieces, x_ref, w_ref, cos_ref, sin_ref, new_ref, wq_ref,
                 out_ref, new_out_ref,
                 x_other, w_all, arrived, leaving, total,
                 x_send, x_recv, w_send, w_recv, sum_send, sum_recv,
                 new_all, near_out, near_in, far_in, *relay_sems):
    members = 2 * chips
    bits = (groups - 1).bit_length()
    f = lax.axis_index("fsdp")
    t = lax.axis_index("tp")
    c = lax.div(t, 2)
    e = lax.rem(t, 2)
    token_count = x_ref.shape[0]
    rows = token_count // pieces
    own = out_ref.shape[1]
    table_rows = cos_ref.shape[0]
    gather, multiply, scatter, collect, drain = relay(
        f, t, groups, members, new_ref, new_all, near_out, near_in, far_in, relay_sems)

    def piece(k):
        return pl.ds(pl.multiple_of(k * rows, rows), rows)

    def half(which):
        return pl.ds(pl.multiple_of(which * own, own), own)

    def x_copy(k):
        return pltpu.make_async_remote_copy(
            src_ref=x_ref.at[piece(k)], dst_ref=x_other.at[piece(k)],
            send_sem=x_send.at[k], recv_sem=x_recv.at[k],
            device_id=(f, 2 * c + 1 - e), device_id_type=MESH)

    def w_copy(j, swap):
        core = e if swap == 0 else 1 - e
        return pltpu.make_async_remote_copy(
            src_ref=w_ref.at[:, half(core)], dst_ref=w_all.at[j, swap],
            send_sem=w_send.at[j, swap], recv_sem=w_recv.at[j, swap],
            device_id=(flip(f, j, bits), 2 * c + core), device_id_type=MESH)

    def sum_copy(j, k, slot, chip):
        return pltpu.make_async_remote_copy(
            src_ref=leaving.at[j, piece(k)], dst_ref=arrived.at[slot, piece(k)],
            send_sem=sum_send.at[j, k], recv_sem=sum_recv.at[slot, k],
            device_id=(f, 2 * chip + e), device_id_type=MESH)

    def send_right(j, k):
        sum_copy(j, k, j, c + 1).start()

    def send_left(j, k, d):
        @pl.when(d == c - 1)
        def _():
            sum_copy(j, k, groups, c - 1).start()

        @pl.when(d < c - 1)
        def _():
            sum_copy(j, k, j, c - 1).start()

    def add_arrived(j, k):
        sum_copy(j, k, j, c).wait_recv()
        leaving[j, piece(k)] = (
            leaving[j, piece(k)].astype(jnp.float32) + arrived[j, piece(k)].astype(jnp.float32)
        ).astype(jnp.bfloat16)

    barrier = pltpu.get_barrier_semaphore()
    for j in range(1, groups):
        for core in range(2):
            pl.semaphore_signal(barrier, inc=1, device_id=(flip(f, j, bits), 2 * c + core),
                                device_id_type=MESH)
    for i in range(1, members):
        pl.semaphore_signal(barrier, inc=1, device_id=(f, lax.rem(t + i, members)),
                            device_id_type=MESH)
    pl.semaphore_wait(barrier, 2 * (groups - 1) + members - 1)

    direct = [j for j in range(1, groups) if j & (j - 1) == 0]
    w_copy(0, 1).start()
    for j in direct:
        for swap in range(2):
            w_copy(j, swap).start()

    @pl.loop(0, pieces)
    def _(k):
        x_copy(k).start()

    gather()
    w_all[0, 0] = w_ref[:, half(e)]
    w_copy(0, 1).wait_recv()

    @pl.loop(0, groups)
    def _(j):
        d = flip(f, j, bits)

        @pl.when(j == 1)
        def _():
            multiply([wq_ref, w_ref])

        @pl.when(j == groups - 1)
        def _():
            scatter()

        @pl.when(j > 0)
        def _():
            for swap in range(2):
                pltpu.make_async_remote_copy(
                    src_ref=w_ref.at[:, half(0)], dst_ref=w_all.at[j, swap],
                    send_sem=w_send.at[j, swap], recv_sem=w_recv.at[j, swap],
                    device_id=(f, 2 * c + 1 - e), device_id_type=MESH).wait_recv()

        @pl.when(j == 1)
        def _():
            for later in range(1, groups):
                if later not in direct:
                    for swap in range(2):
                        w_copy(later, swap).start()

        @pl.loop(0, pieces)
        def _(k):
            @pl.when(j == 0)
            def _():
                x_copy(k).wait_recv()

            term = jnp.dot(x_ref[piece(k)], w_all[j, 0], preferred_element_type=jnp.float32)
            term += jnp.dot(x_other[piece(k)], w_all[j, 1], preferred_element_type=jnp.float32)

            @pl.when(d == c)
            def _():
                total[piece(k)] = term

            @pl.when(d != c)
            def _():
                leaving[j, piece(k)] = term.astype(jnp.bfloat16)

                @pl.when(c == 0)
                def _():
                    send_right(j, k)

                @pl.when(c == chips - 1)
                def _():
                    send_left(j, k, d)

    mine = flip(f, c, bits)
    from_right = flip(f, 0, bits)
    from_left = flip(f, chips - 1, bits)
    slot_right = mine - jnp.where(from_right < mine, 1, 0)
    slot_left = mine - jnp.where(from_left < mine, 1, 0)
    last = jnp.where(c == 0, slot_left, jnp.where(c == chips - 1, slot_right,
                                                  jnp.maximum(slot_left, slot_right)))

    def finish(k):
        @pl.when(c > 0)
        def _():
            sum_copy(mine, k, mine, c).wait_recv()
            total[piece(k)] += arrived[mine, piece(k)].astype(jnp.float32)

        @pl.when(c < chips - 1)
        def _():
            sum_copy(mine, k, groups, c).wait_recv()
            total[piece(k)] += arrived[groups, piece(k)].astype(jnp.float32)

        place = pl.ds(pl.multiple_of(lax.rem(k * rows, table_rows), rows), rows)
        for b in range(own // HD):
            cut = slice(b * HD, (b + 1) * HD)
            value = total[piece(k), cut]
            turned = value * cos_ref[place, cut] + pltpu.roll(value, HD // 2, 1) * sin_ref[place, cut]
            out_ref[piece(k), cut] = turned.astype(out_ref.dtype)

    count = (chips - 1) * pieces

    def at(step, distance):
        index = step - SKEW * distance
        known = jnp.minimum(jnp.maximum(index, 0), count - 1)
        valid = jnp.logical_and(index >= 0, index < count)
        return valid, lax.div(known, pieces), lax.rem(known, pieces)

    @pl.loop(0, count + SKEW * (chips - 1))
    def _(step):
        valid, slot, k_right = at(step, c)
        j_right = slot + jnp.where(from_right <= slot, 1, 0)
        d_right = flip(f, j_right, bits)

        @pl.when(jnp.logical_and(valid, jnp.logical_and(c > 0, d_right > c)))
        def _():
            add_arrived(j_right, k_right)
            send_right(j_right, k_right)

        valid, slot, k_left = at(step, chips - 1 - c)
        j_left = slot + jnp.where(from_left <= slot, 1, 0)
        d_left = flip(f, j_left, bits)

        @pl.when(jnp.logical_and(valid, jnp.logical_and(c < chips - 1, d_left < c)))
        def _():
            add_arrived(j_left, k_left)
            send_left(j_left, k_left, d_left)

        valid, slot, k_own = at(step, chips - 1)

        @pl.when(jnp.logical_and(valid, slot == last))
        def _():
            finish(k_own)

    new_out_ref[...] = collect()
    drain()
    w_copy(0, 1).wait_send()
    for j in range(1, groups):
        for swap in range(2):
            w_copy(j, swap).wait_send()

    @pl.loop(0, pieces)
    def _(k):
        x_copy(k).wait_send()

        @pl.loop(0, groups)
        def _(j):
            @pl.when(flip(f, j, bits) != c)
            def _():
                sum_copy(j, k, j, c).wait_send()


def recompute_cache(prefix_states, w_keyvalue, cosine, sine_part, new_states, w_query):
    groups, members = lax.axis_size("fsdp"), lax.axis_size("tp")
    chips = members // 2
    assert chips == groups and groups & (groups - 1) == 0
    token_count, depth = prefix_states.shape
    own = w_keyvalue.shape[1] // 2
    pieces = token_count // 256
    fresh_count = new_states.shape[0]
    fresh_width = (w_query.shape[1] + w_keyvalue.shape[1]) * groups // members
    return pl.pallas_call(
        functools.partial(cache_kernel, groups, chips, pieces),
        out_shape=(
            jax.ShapeDtypeStruct((token_count, own), jnp.bfloat16),
            jax.ShapeDtypeStruct((fresh_count, fresh_width), jnp.float32),
        ),
        in_specs=[VMEM] * 6,
        out_specs=(VMEM, VMEM),
        scratch_shapes=[
            pltpu.VMEM((token_count, depth), jnp.bfloat16),
            pltpu.VMEM((groups, 2, depth, own), jnp.bfloat16),
            pltpu.VMEM((groups + 1, token_count, own), jnp.bfloat16),
            pltpu.VMEM((groups, token_count, own), jnp.bfloat16),
            pltpu.VMEM((token_count, own), jnp.float32),
            pltpu.SemaphoreType.DMA((pieces,)),
            pltpu.SemaphoreType.DMA((pieces,)),
            pltpu.SemaphoreType.DMA((groups, 2)),
            pltpu.SemaphoreType.DMA((groups, 2)),
            pltpu.SemaphoreType.DMA((groups, pieces)),
            pltpu.SemaphoreType.DMA((groups + 1, pieces)),
        ] + relay_scratch(groups, members, fresh_count, depth, fresh_width),
        compiler_params=pltpu.CompilerParams(
            collective_id=0, has_side_effects=True, vmem_limit_bytes=60 * 1024 * 1024),
    )(prefix_states, w_keyvalue, cosine, sine_part, new_states, w_query)


def project_kernel(groups, members, x_ref, w_ref, out_ref, x_all, near_out, near_in, far_in, *sems):
    f = lax.axis_index("fsdp")
    t = lax.axis_index("tp")
    barrier = pltpu.get_barrier_semaphore()
    for j in range(1, groups):
        pl.semaphore_signal(barrier, inc=1, device_id=(lax.rem(f + j, groups), t),
                            device_id_type=MESH)
    for i in range(1, members):
        pl.semaphore_signal(barrier, inc=1, device_id=(f, lax.rem(t + i, members)),
                            device_id_type=MESH)
    pl.semaphore_wait(barrier, groups + members - 2)
    gather, multiply, scatter, collect, drain = relay(
        f, t, groups, members, x_ref, x_all, near_out, near_in, far_in, sems)
    gather()
    multiply([w_ref])
    scatter()
    out_ref[...] = collect().astype(out_ref.dtype)
    drain()


def project(x, weight, out_dtype, collective_id):
    groups, members = lax.axis_size("fsdp"), lax.axis_size("tp")
    rows, depth = x.shape
    columns = weight.shape[1] * groups // members
    return pl.pallas_call(
        functools.partial(project_kernel, groups, members),
        out_shape=jax.ShapeDtypeStruct((rows, columns), out_dtype),
        in_specs=[VMEM] * 2,
        out_specs=VMEM,
        scratch_shapes=relay_scratch(groups, members, rows, depth, columns),
        compiler_params=pltpu.CompilerParams(
            collective_id=collective_id, has_side_effects=True, vmem_limit_bytes=32 * 1024 * 1024),
    )(x, weight)


def body(prefix_states, new_states, w_query, w_keyvalue, w_output, lengths):
    my_index = lax.axis_index("tp")
    token_count = prefix_states.shape[0]
    fresh_count = new_states.shape[0]
    seq_lengths = lengths[0]
    score_scale = HD ** (-0.5)
    own_rows = w_keyvalue.shape[1] // 2
    block_count = own_rows // HD
    block_kind = (my_index * block_count + jnp.arange(block_count, dtype=jnp.int32)) % 2
    frequency = theta_base ** (-2.0 * jnp.arange(HD // 2, dtype=jnp.float32) / HD)
    angles = jnp.arange(L, dtype=jnp.int32).astype(jnp.float32)[:, None] * frequency[None, :]
    cosine, sine_part = jnp.cos(angles), jnp.sin(angles)
    is_key = jnp.repeat(block_kind == 0, HD)[None, :]
    cosine = jnp.where(is_key, jnp.tile(cosine, (1, 2 * block_count)), 1.0)
    sine_part = jnp.where(
        is_key, jnp.tile(jnp.concatenate([-sine_part, sine_part], axis=1), (1, block_count)), 0.0
    )
    cache_out, new_sum = recompute_cache(
        prefix_states, w_keyvalue, cosine, sine_part, new_states, w_query
    )
    query_width = new_sum.shape[1] - own_rows
    query_sum, fresh_sum = new_sum[:, :query_width], new_sum[:, query_width:]
    fresh_positions = (
        jnp.repeat(seq_lengths, STEPS) + jnp.tile(jnp.arange(STEPS, dtype=jnp.int32), NSEQ)
    ).astype(jnp.float32)
    fresh_blocks = fresh_sum.reshape(fresh_count, block_count, HD)
    fresh_rotated = rotate(fresh_blocks, fresh_positions)
    fresh_mine = jnp.where((block_kind == 0)[None, :, None], fresh_rotated, fresh_blocks).astype(
        jnp.bfloat16
    )
    if block_count == 1:
        cache_other, fresh_other = partner((cache_out, fresh_mine), "tp", 0)
        holds_keys = my_index % 2 == 0
        key_table = jnp.where(holds_keys, cache_out, cache_other)
        value_table = jnp.where(holds_keys, cache_other, cache_out)
        fresh_keys = jnp.where(holds_keys, fresh_mine[:, 0], fresh_other[:, 0])
        fresh_values = jnp.where(holds_keys, fresh_other[:, 0], fresh_mine[:, 0])
    else:
        key_table = cache_out[:, :HD]
        value_table = cache_out[:, HD:]
        fresh_keys = fresh_mine[:, 0]
        fresh_values = fresh_mine[:, 1]
    local_heads = query_sum.shape[1] // HD
    query_rot = rotate(query_sum.reshape(fresh_count, local_heads, HD), fresh_positions).astype(
        jnp.bfloat16
    )
    query_four = query_rot.reshape(NSEQ, STEPS, local_heads, HD)
    prefix_scores = (
        jnp.einsum(
            "sjhd,sld->sjhl",
            query_four,
            key_table.reshape(NSEQ, L, HD),
            preferred_element_type=jnp.float32,
        )
        * score_scale
    )
    live_keys = jnp.arange(L, dtype=jnp.int32)[None, :] < seq_lengths[:, None]
    prefix_scores = jnp.where(live_keys[:, None, None, :], prefix_scores, masked_score)
    fresh_scores = (
        jnp.einsum(
            "sjhd,sid->sjhi",
            query_four,
            fresh_keys.reshape(NSEQ, STEPS, HD),
            preferred_element_type=jnp.float32,
        )
        * score_scale
    )
    causal = jnp.arange(STEPS)[None, :] <= jnp.arange(STEPS)[:, None]
    fresh_scores = jnp.where(causal[None, :, None, :], fresh_scores, masked_score)
    row_max = jnp.maximum(jnp.max(prefix_scores, axis=-1), jnp.max(fresh_scores, axis=-1))
    prefix_weight = jnp.exp(prefix_scores - row_max[..., None])
    fresh_weight = jnp.exp(fresh_scores - row_max[..., None])
    denominator = jnp.sum(prefix_weight, axis=-1) + jnp.sum(fresh_weight, axis=-1)
    numerator = jnp.einsum(
        "sjhl,sld->sjhd",
        prefix_weight.astype(jnp.bfloat16),
        value_table.reshape(NSEQ, L, HD),
        preferred_element_type=jnp.float32,
    )
    numerator = numerator + jnp.einsum(
        "sjhi,sid->sjhd",
        fresh_weight.astype(jnp.bfloat16),
        fresh_values.reshape(NSEQ, STEPS, HD),
        preferred_element_type=jnp.float32,
    )
    attended = (
        (numerator / denominator[..., None])
        .reshape(fresh_count, local_heads * HD)
        .astype(jnp.bfloat16)
    )
    return (cache_out, project(attended, w_output, jnp.bfloat16, 1))


def solution(mesh):
    in_specs = (
        P("fsdp", "tp"),
        P("fsdp", "tp"),
        P("tp", "fsdp"),
        P("tp", "fsdp"),
        P("tp", "fsdp"),
        P("fsdp", None),
    )
    out_specs = (P("fsdp", "tp"), P("fsdp", "tp"))
    return jax.shard_map(body, mesh=mesh, in_specs=in_specs, out_specs=out_specs, check_vma=False)
```

profile of v0, /device:TPU:1, one launch (start us, length us, event | category | flops | bytes accessed | tf_op | source)
XLA Modules:
  0.0 248.2 jit_solution(14372051280073245072)
XLA Ops:
  0.7 1.0 fusion.9
  1.7 0.2 copy.9
  1.9 0.4 tile.14
  2.3 0.1 tile.12
  2.4 0.3 copy.8
  2.8 1.5 bitcast_select_fusion
  4.3 179.9 %shard_map.77 = (bf16[4096,256]{1,0:T(8,128)(2,1)}, f32[16,1280]{1,0:T(8,128)}) custom-call(bf16[4096,1024]{1,0:T(8,128)(2,1)} %x_ref.1, bf16[1024,512]{1,0:T(8,128)(2,1)} %w_ref.2, f32[1024,256]{1,0:T(8,128)} %get-tuple-element.20.cos_ref, f32[1024,256]{1,0:T(8,128)} %get-tuple-element.19.sin_ref, bf16[16,1024]{1,0:T(8,128)(2,1)} %new_ref.1, ...), custom_call_target="tpu_custom_call" | custom-call | tf_op jit(solution)/shard_map/pallas_call | solution.py:368
  184.2 0.7 copy_bitcast_fusion.1
  185.0 0.1 convert_element_type.39
  185.1 0.1 multiply_cosine_fusion.1
  185.3 0.1 multiply_subtract_fusion
  185.3 0.8 fusion.13
  186.1 0.8 slice_bitcast_fusion
  187.0 0.1 subtract_convert_fusion
  187.1 0.3 fusion.22
  187.5 1.8 fusion.19
  189.3 0.1 iota_compare_fusion
  189.4 0.6 fusion.21
  190.0 0.2 fusion.4
  190.3 0.3 fusion.6
  190.6 0.2 fusion.2
  190.8 55.4 %shard_map.78 = bf16[16,1024]{1,0:T(8,128)(2,1)S(1)} custom-call(bf16[16,1024]{1,0:T(8,128)(2,1)S(1)} %bitcast.49, bf16[1024,2048]{1,0:T(8,128)(2,1)S(1)} %copy-done), custom_call_target="tpu_custom_call" | custom-call | tf_op jit(solution)/shard_map/pallas_call | solution.py:418
  246.3 1.3 copy.29
  247.6 0.6 copy.30
  (19 shorter events, 0.3 us)
Async XLA Ops:
  4.3 180.6 %copy-start.2 = (s32[1,4]{1,0:T(1,128)S(1)}, s32[1,4]{1,0:T(1,128)}, u32[]{:S(2)}) copy-start(s32[1,4]{1,0:T(1,128)} %param.11) | copy-start | bytes 52
  187.5 3.4 %copy-start = (bf16[1024,2048]{1,0:T(8,128)(2,1)S(1)}, bf16[1024,2048]{1,0:T(8,128)(2,1)}, u32[]{:S(2)}) copy-start(bf16[1024,2048]{1,0:T(8,128)(2,1)} %w_ref.3) | copy-start | bytes 12582916
  189.4 56.9 %copy-start.1 = (bf16[4096,256]{1,0:T(8,128)(2,1)S(1)}, bf16[4096,256]{1,0:T(8,128)(2,1)}, u32[]{:S(2)}) copy-start(bf16[4096,256]{1,0:T(8,128)(2,1)} %get-tuple-element.27) | copy-start | bytes 6291460
where the time goes:
time: 249 us; the launch traced here: 248 us
  Pallas kernels  235 us (94%)
  local copies, waits for them, and re-layouts  6.53 us (3%)
  other arithmetic  4.09 us (2%)
    pallas_call x1, Pallas kernels, recompute_cache(): pl.pallas_call(functools.partial(cache_kernel, groups, chips, pieces), ou...  180 us
    pallas_call x1, Pallas kernels, project(): pl.pallas_call(functools.partial(project_kernel, groups, members), out_sh...  55.4 us

commit v1 on v0

--- a/solution.py
+++ b/solution.py
@@ -12,6 +12,7 @@
 L = 1024
 STEPS = 4
 SKEW = 2
+WINDOW = 3
 MESH = pl.DeviceIdType.MESH
 VMEM = pl.BlockSpec(memory_space=pltpu.VMEM)
 
@@ -223,6 +224,8 @@
         x_copy(k).start()
 
     gather()
+    at_end = jnp.logical_or(c == 0, c == chips - 1)
+    omitted = jnp.where(c == 0, flip(f, 0, bits), flip(f, chips - 1, bits))
     w_all[0, 0] = w_ref[:, half(e)]
     w_copy(0, 1).wait_recv()
 
@@ -269,6 +272,14 @@
             @pl.when(d != c)
             def _():
                 leaving[j, piece(k)] = term.astype(jnp.bfloat16)
+                earlier = (j - jnp.where(omitted < j, 1, 0)) * pieces + k - WINDOW
+
+                @pl.when(jnp.logical_and(at_end, earlier >= 0))
+                def _():
+                    sent = jnp.maximum(earlier, 0)
+                    slot = lax.div(sent, pieces)
+                    sum_copy(slot + jnp.where(omitted <= slot, 1, 0), lax.rem(sent, pieces),
+                             0, c).wait_send()
 
                 @pl.when(c == 0)
                 def _():
@@ -351,7 +362,10 @@
 
         @pl.loop(0, groups)
         def _(j):
-            @pl.when(flip(f, j, bits) != c)
+            index = (j - jnp.where(omitted < j, 1, 0)) * pieces + k
+            waiting = jnp.logical_or(jnp.logical_not(at_end), index >= (chips - 1) * pieces - WINDOW)
+
+            @pl.when(jnp.logical_and(flip(f, j, bits) != c, waiting))
             def _():
                 sum_copy(j, k, j, c).wait_send()
 

time: 249 us -> 249 us (level)
  no operation moved by 1% of the time
where the time goes in v1:
time: 249 us
  Pallas kernels  236 us (95%)
  local copies, waits for them, and re-layouts  6.53 us (3%)
  other arithmetic  4.09 us (2%)
    pallas_call x1, Pallas kernels, recompute_cache(): pl.pallas_call(functools.partial(cache_kernel, groups, chips, pieces), ou...  180 us
    pallas_call x1, Pallas kernels, project(): pl.pallas_call(functools.partial(project_kernel, groups, members), out_sh...  55.8 us

profile of v1, /device:TPU:1, one launch (start us, length us, event | category | flops | bytes accessed | tf_op | source)
XLA Modules:
  0.0 248.6 jit_solution(5789022949541636248)
XLA Ops:
  0.7 1.0 fusion.9
  1.7 0.2 copy.9
  1.9 0.4 tile.14
  2.3 0.1 tile.12
  2.4 0.3 copy.8
  2.8 1.5 bitcast_select_fusion
  4.3 179.9 %shard_map.77 = (bf16[4096,256]{1,0:T(8,128)(2,1)}, f32[16,1280]{1,0:T(8,128)}) custom-call(bf16[4096,1024]{1,0:T(8,128)(2,1)} %x_ref.1, bf16[1024,512]{1,0:T(8,128)(2,1)} %w_ref.2, f32[1024,256]{1,0:T(8,128)} %get-tuple-element.20.cos_ref, f32[1024,256]{1,0:T(8,128)} %get-tuple-element.19.sin_ref, bf16[16,1024]{1,0:T(8,128)(2,1)} %new_ref.1, ...), custom_call_target="tpu_custom_call" | custom-call | tf_op jit(solution)/shard_map/pallas_call | solution.py:382
  184.3 0.7 copy_bitcast_fusion.1
  185.1 0.1 convert_element_type.39
  185.1 0.1 multiply_cosine_fusion.1
  185.3 0.1 multiply_subtract_fusion
  185.3 0.8 fusion.13
  186.1 0.8 slice_bitcast_fusion
  187.0 0.1 subtract_convert_fusion
  187.1 0.3 fusion.22
  187.5 1.8 fusion.19
  189.3 0.1 iota_compare_fusion
  189.4 0.6 fusion.21
  190.0 0.2 fusion.4
  190.3 0.3 fusion.6
  190.6 0.2 fusion.2
  190.9 55.8 %shard_map.78 = bf16[16,1024]{1,0:T(8,128)(2,1)S(1)} custom-call(bf16[16,1024]{1,0:T(8,128)(2,1)S(1)} %bitcast.49, bf16[1024,2048]{1,0:T(8,128)(2,1)S(1)} %copy-done), custom_call_target="tpu_custom_call" | custom-call | tf_op jit(solution)/shard_map/pallas_call | solution.py:432
  246.6 1.3 copy.29
  248.0 0.6 copy.30
  (19 shorter events, 0.3 us)
Async XLA Ops:
  4.3 180.7 %copy-start.2 = (s32[1,4]{1,0:T(1,128)S(1)}, s32[1,4]{1,0:T(1,128)}, u32[]{:S(2)}) copy-start(s32[1,4]{1,0:T(1,128)} %param.11) | copy-start | bytes 52
  187.5 3.4 %copy-start = (bf16[1024,2048]{1,0:T(8,128)(2,1)S(1)}, bf16[1024,2048]{1,0:T(8,128)(2,1)}, u32[]{:S(2)}) copy-start(bf16[1024,2048]{1,0:T(8,128)(2,1)} %w_ref.3) | copy-start | bytes 12582916
  189.4 57.2 %copy-start.1 = (bf16[4096,256]{1,0:T(8,128)(2,1)S(1)}, bf16[4096,256]{1,0:T(8,128)(2,1)}, u32[]{:S(2)}) copy-start(bf16[4096,256]{1,0:T(8,128)(2,1)} %get-tuple-element.27) | copy-start | bytes 6291460
